TPU v7x, 32 devices: a whole 2x2x4 slice. The times are simulated.
32 devices in a mesh: cp: 4 (over y, x), ep: 8 (over z, core).
Axes of the slice: x: 2, y: 2, z: 4, core: 2. Of those that a mesh axis runs over, the one named last changes fastest.
Arguments:
- tokens: bfloat16 [8, 256, 3584], P('ep', 'cp'), may hold values from -6 to 6
- cotangent: bfloat16 [8, 256, 3584], P('ep', 'cp'), may hold values from -6 to 6
- routes: int32 [8, 256, 8], P('ep', 'cp'), may hold values from 0 to 31, all different within a row; in each aligned block of 64 rows (0 to 63, 64 to 127, ..., all dimensions but the last counted through in order) at most 20 rows name the same one
- router_weights: float32 [8, 256, 8], P('ep', 'cp'), may hold values from 0.02 to 0.5
- w_gate: bfloat16 [32, 3584, 1024], P(('cp', 'ep')), may hold values from -0.09375 to 0.09375
- w_up: bfloat16 [32, 3584, 1024], P(('cp', 'ep')), may hold values from -0.09375 to 0.09375
- w_down: bfloat16 [32, 1024, 3584], P(('cp', 'ep')), may hold values from -0.1875 to 0.1875
Outputs:
- layer_out: bfloat16 [8, 256, 3584], P('ep', 'cp')
- token_grad: bfloat16 [8, 256, 3584], P('ep', 'cp')
- gate_grad: float32 [8, 256, 8], P('ep', 'cp')
Inputs may be any that keep to these rules, and one draw needn't show every extreme that they name: `routes`: each row names 8 distinct experts; in each aligned block of 64 rows (the rows of one device) no expert is named by more than 20 of the block's slots.
All inputs are finite; a program needn't handle non-finite values.
Results may differ from a plain program's by a relative error of at most 0.0058.
Values may be sent and summed in bfloat16 or wider, within the bound.
A program may use at most 128 MiB of HBM per device.

v0:
```python
import jax
import jax.numpy as jnp
from jax import lax
from jax.sharding import PartitionSpec as P


def expert_rows(stacked, gate_matrix, up_matrix, down_matrix):
    inputs = stacked[:, 0]
    grad_in = stacked[:, 1]
    gate_pre = jnp.dot(inputs, gate_matrix, preferred_element_type=jnp.float32)
    up_pre = jnp.dot(inputs, up_matrix, preferred_element_type=jnp.float32)
    sig_gate = jax.nn.sigmoid(gate_pre)
    silu_gate = gate_pre * sig_gate
    hidden = (silu_gate * up_pre).astype(jnp.bfloat16)
    expert_out = jnp.dot(hidden, down_matrix, preferred_element_type=jnp.float32).astype(
        jnp.bfloat16
    )
    grad_hidden = jnp.dot(grad_in, down_matrix.T, preferred_element_type=jnp.float32)
    grad_gate = (grad_hidden * up_pre * sig_gate * (1.0 + gate_pre * (1.0 - sig_gate))).astype(
        jnp.bfloat16
    )
    grad_up = (grad_hidden * silu_gate).astype(jnp.bfloat16)
    expert_grad = (
        jnp.dot(grad_gate, gate_matrix.T, preferred_element_type=jnp.float32)
        + jnp.dot(grad_up, up_matrix.T, preferred_element_type=jnp.float32)
    ).astype(jnp.bfloat16)
    return jnp.stack([expert_out, expert_grad], 1)


def per_device(tokens, cotangent, routes, router_weights, w_gate, w_up, w_down):
    cp_count = lax.axis_size("cp")
    ep_count = lax.axis_size("ep")
    owners = cp_count * ep_count
    positions = tokens.shape[1]
    features = tokens.shape[2]
    top_k = routes.shape[2]
    capacity = positions * top_k // owners * 5 // 4
    gate_matrix = w_gate[0]
    up_matrix = w_up[0]
    down_matrix = w_down[0]
    flat_routes = routes[0].reshape(positions * top_k)
    one_hot = (flat_routes[:, None] == jnp.arange(owners, dtype=jnp.int32)[None, :]).astype(
        jnp.int32
    )
    before = jnp.cumsum(one_hot, axis=0) - one_hot
    ranking = jnp.sum(before * one_hot, axis=1)
    dest_slot = flat_routes * capacity + ranking
    token_of = jnp.arange(positions * top_k, dtype=jnp.int32) // top_k
    slot_token = jnp.full((owners * capacity,), positions, jnp.int32).at[dest_slot].set(token_of)
    stacked = jnp.concatenate(
        [jnp.stack([tokens[0], cotangent[0]], 1), jnp.zeros((1, 2, features), jnp.bfloat16)], 0
    )
    send_rows = stacked[slot_token]
    received = lax.all_to_all(
        send_rows.reshape(owners, capacity, 2, features),
        ("cp", "ep"),
        split_axis=0,
        concat_axis=0,
        tiled=True,
    )
    outcome = expert_rows(received.reshape(-1, 2, features), gate_matrix, up_matrix, down_matrix)
    returned = lax.all_to_all(
        outcome.reshape(received.shape), ("cp", "ep"), split_axis=0, concat_axis=0, tiled=True
    )
    fetched = returned.reshape(owners * capacity, 2, features)[dest_slot]
    expert_out = fetched[:, 0].reshape(positions, top_k, features).astype(jnp.float32)
    expert_grad = fetched[:, 1].reshape(positions, top_k, features).astype(jnp.float32)
    mixing = router_weights[0]
    layer_out = jnp.einsum("tk,tkd->td", mixing, expert_out, precision=lax.Precision.HIGHEST)
    token_grad = jnp.einsum("tk,tkd->td", mixing, expert_grad, precision=lax.Precision.HIGHEST)
    gate_grad = jnp.sum(cotangent[0].astype(jnp.float32)[:, None, :] * expert_out, axis=-1)
    return (
        layer_out.astype(jnp.bfloat16)[None],
        token_grad.astype(jnp.bfloat16)[None],
        gate_grad[None],
    )


def solution(mesh):
    in_specs = (
        P("ep", "cp", None),
        P("ep", "cp", None),
        P("ep", "cp", None),
        P("ep", "cp", None),
        P(("cp", "ep"), None, None),
        P(("cp", "ep"), None, None),
        P(("cp", "ep"), None, None),
    )
    out_specs = (P("ep", "cp", None), P("ep", "cp", None), P("ep", "cp", None))
    return jax.shard_map(
        per_device, mesh=mesh, in_specs=in_specs, out_specs=out_specs, check_vma=False
    )
```

profile of v0, /device:TPU:0, one launch (start us, length us, event | category | flops | bytes accessed | tf_op | source)
XLA Modules:
  0.0 655.5 jit_solution(1782279453990308819)
XLA Ops:
  0.6 0.8 copy.27
  1.4 0.1 eq.29
  1.5 0.1 eq.25
  1.6 0.7 broadcast_multiply_fusion
  2.3 1.2 reduce-window.6
  3.5 0.2 slice_reduce_fusion
  3.7 0.1 copy.26
  3.8 0.1 mul.53
  3.9 0.1 fusion.40
  4.0 2.4 scatter_custom_fusion
  6.5 1.7 copy.24
  8.2 1.7 copy.25
  10.0 2.1 fusion.33
  12.1 31.5 %gather_fusion = bf16[640,2,3584]{2,1,0:T(2,128)(2,1)} fusion(bf16[65,2,3584]{2,1,0:T(2,128)(2,1)S(1)} %fusion.33, s32[1024]{0:T(1024)S(1)} %pad_clamp_fusion.1), kind=kCustom, calls=%fused_computation | custom fusion | bytes 18352640 | tf_op jit(solution)/shard_map/gather | solution.py:53
  43.6 209.2 %all_to_all.10 = bf16[32,20,2,3584]{3,2,1,0:T(2,128)(2,1)S(1)} all-to-all(bf16[32,20,2,3584]{3,2,1,0:T(2,128)(2,1)} %bitcast.79), channel_id=1, replica_groups=mesh['cp'=4,'ep'=8] {'cp','ep'}, dimensions={0} | all-to-all | bytes 18350080 | tf_op jit(solution)/shard_map/all_to_all | solution.py:54
  252.9 13.7 %fusion.50 = (bf16[640,1,3584]{2,1,0:T(2,128)(2,1)}, bf16[640,1,3584]{2,1,0:T(2,128)(2,1)S(1)}) fusion(bf16[640,2,3584]{2,1,0:T(2,128)(2,1)S(1)} %bitcast.78), kind=kLoop, calls=%fused_computation.72 | loop fusion | bytes 18350080 | tf_op jit(solution)/shard_map/slice | solution.py:8
  266.6 9.8 %fusion.10 = f32[640,1024]{1,0:T(8,128)S(1)} fusion(bf16[1,3584,1024]{2,1,0:T(8,128)(2,1)} %param.11, bf16[640,1,3584]{2,1,0:T(2,128)(2,1)} %get-tuple-element.12), kind=kOutput, calls=%fused_computation.15 | convolution fusion | flops 4697620480 | bytes 14548992 | tf_op jit(solution)/shard_map/dot_general | solution.py:10
  276.3 0.0 copy-done.1
  276.3 0.0 copy-start.4
  276.4 9.6 %fusion.6 = f32[640,1024]{1,0:T(8,128)} fusion(bf16[1,3584,1024]{2,1,0:T(8,128)(2,1)} %param.12, bf16[640,1,3584]{2,1,0:T(2,128)(2,1)S(1)} %copy-done.1), kind=kOutput, calls=%fused_computation.11 | convolution fusion | flops 4697620480 | bytes 14548992 | tf_op jit(solution)/shard_map/dot_general | solution.py:11
  286.0 8.7 %fusion = f32[640,1024]{1,0:T(8,128)} fusion(bf16[1,1024,3584]{2,1,0:T(8,128)(2,1)} %param.13, bf16[640,1,3584]{2,1,0:T(2,128)(2,1)S(1)} %get-tuple-element.13), kind=kOutput, calls=%fused_computation.5 | convolution fusion | flops 4697620480 | bytes 14548992 | tf_op jit(solution)/shard_map/dot_general | solution.py:18
  294.7 12.5 %fusion.4 = f32[640,3584]{1,0:T(8,128)} fusion(bf16[1,3584,1024]{2,1,0:T(8,128)(2,1)} %param.12, f32[640,1024]{1,0:T(8,128)} %fusion, f32[640,1024]{1,0:T(8,128)S(1)} %fusion.10), kind=kOutput, calls=%fused_computation.9 | convolution fusion | flops 4701552640 | bytes 21757952 | tf_op jit(solution)/shard_map/dot_general | solution.py:25
  307.2 0.0 copy-done.4
  307.2 0.0 copy-done.5
  307.2 10.1 %fusion.12 = bf16[640,3584]{1,0:T(8,128)(2,1)} fusion(bf16[1,1024,3584]{2,1,0:T(8,128)(2,1)} %param.13, f32[640,1024]{1,0:T(8,128)S(1)} %copy-done.5, f32[640,1024]{1,0:T(8,128)S(1)} %fusion.10), kind=kOutput, calls=%fused_computation.18 | convolution fusion | flops 4703846400 | bytes 17170432 | tf_op jit(solution)/shard_map/dot_general | solution.py:15
  317.4 15.7 %add_convert_fusion = bf16[640,3584]{1,0:T(8,128)(2,1)} fusion(f32[640,3584]{1,0:T(8,128)} %fusion.4, bf16[1,3584,1024]{2,1,0:T(8,128)(2,1)} %param.11, f32[640,1024]{1,0:T(8,128)} %copy-done.4, f32[640,1024]{1,0:T(8,128)} %fusion, f32[640,1024]{1,0:T(8,128)} %fusion.6), kind=kOutput, calls=%fused_computation.4 | convolution fusion | flops 4708761600 | bytes 28966912 | tf_op jit(solution)/shard_map/dot_general | solution.py:24
  333.0 7.2 %stack.14 = bf16[32,20,1,3584]{3,1,0,2:T(8,128)(2,1)} reshape(bf16[640,3584]{1,0:T(8,128)(2,1)} %add_convert_fusion) | data formatting | bytes 9175040 | tf_op jit(solution)/shard_map/stack | solution.py:27
  340.3 7.3 %stack.13 = bf16[32,20,1,3584]{3,1,0,2:T(8,128)(2,1)} reshape(bf16[640,3584]{1,0:T(8,128)(2,1)} %fusion.12) | data formatting | bytes 9175040 | tf_op jit(solution)/shard_map/stack | solution.py:27
  347.6 6.5 pad_maximum_fusion
  354.0 8.4 %copy.30 = bf16[32,20,2,3584]{3,2,1,0:T(2,128)(2,1)} copy(bf16[32,20,2,3584]{3,1,0,2:T(8,128)(2,1)S(1)} %pad_maximum_fusion) | data formatting | bytes 18350080 | tf_op jit(solution)/shard_map/stack | solution.py:27
  362.4 4.0 all-to-all-start.1
  366.4 0.0 copy-done.3
  366.4 0.1 copy.32
  366.5 0.0 copy-done.2
  366.5 0.1 bitcast_convert_fusion.2
  366.6 3.8 mul.62
  370.4 11.7 %mul.63 = f32[512,1,3584]{2,1,0:T(1,128)} reshape(f32[64,8,3584]{2,1,0:T(8,128)} %mul.62) | data formatting | bytes 14680064 | tf_op jit(solution)/shard_map/mul | solution.py:71
  382.2 186.0 %all-to-all-done.1 = bf16[32,20,2,3584]{3,2,1,0:T(2,128)(2,1)} async-done(((bf16[32,20,2,3584]{3,2,1,0:T(2,128)(2,1)}), bf16[32,20,2,3584]{3,2,1,0:T(2,128)(2,1)}, u32[]{:S(2)}, u32[]{:S(2)}) %all-to-all-start.1) | async-done | bytes 9175072 | tf_op jit(solution)/shard_map/all_to_all | solution.py:62
  568.2 29.4 %gather_fusion.1 = bf16[512,2,3584]{2,1,0:T(2,128)(2,1)} fusion(bf16[640,2,3584]{2,1,0:T(2,128)(2,1)} %bitcast.10, s32[1024]{0:T(1024)S(1)} %pad_clamp_fusion), kind=kCustom, calls=%fused_computation.1 | custom fusion | bytes 14682112 | tf_op jit(solution)/shard_map/gather | solution.py:65
  597.6 15.4 %fusion.51 = (bf16[512,1,3584]{2,1,0:T(2,128)(2,1)}, bf16[512,1,3584]{2,1,0:T(2,128)(2,1)S(1)}) fusion(bf16[512,2,3584]{2,1,0:T(2,128)(2,1)} %gather_fusion.1), kind=kLoop, calls=%fused_computation.73 | loop fusion | bytes 14680064 | tf_op jit(solution)/shard_map/slice | solution.py:67
  613.0 0.0 copy-start
  613.0 7.3 %fusion.21 = bf16[64,1,3584]{2,1,0:T(2,128)(2,1)} fusion(f32[64,8,1]{1,2,0:T(1,128)S(1)} %copy.32, bf16[512,1,3584]{2,1,0:T(2,128)(2,1)} %get-tuple-element.14), kind=kOutput, calls=%fused_computation.23 | convolution fusion | flops 22020096 | bytes 4130816 | tf_op jit(solution)/shard_map/tk,tkd->td/dot_general | solution.py:70
  620.3 4.1 fusion.24
  624.4 0.0 slice-done.1
  624.4 27.7 %multiply_reduce_fusion = f32[512]{0:T(512)S(1)} fusion(f32[512,1,3584]{2,1,0:T(1,128)S(1)} %bitcast.81, bf16[512,2,3584]{2,1,0:T(2,128)(2,1)S(1)} %copy-done), kind=kLoop, calls=%fused_computation.17 | loop fusion | flops 5504512 | bytes 11012096 | tf_op jit(solution)/shard_map/reduce_sum | solution.py:71
  652.0 0.1 broadcast_in_dim.24
  652.1 0.7 copy.31
  652.8 2.5 fusion.34
  (17 shorter events, 0.1 us)
Async XLA Ops:
  266.6 9.8 %copy-start.1 = (bf16[640,1,3584]{2,1,0:T(2,128)(2,1)S(1)}, bf16[640,1,3584]{2,1,0:T(2,128)(2,1)}, u32[]{:S(2)}) copy-start(bf16[640,1,3584]{2,1,0:T(2,128)(2,1)} %get-tuple-element.12) | copy-start | bytes 13762564
  276.3 30.9 %copy-start.4 = (f32[640,1024]{1,0:T(8,128)}, f32[640,1024]{1,0:T(8,128)S(1)}, u32[]{:S(2)}) copy-start(f32[640,1024]{1,0:T(8,128)S(1)} %fusion.10) | copy-start | bytes 7864324
  294.7 12.5 %copy-start.5 = (f32[640,1024]{1,0:T(8,128)S(1)}, f32[640,1024]{1,0:T(8,128)}, u32[]{:S(2)}) copy-start(f32[640,1024]{1,0:T(8,128)} %fusion.6) | copy-start | bytes 7864324
  362.4 4.0 copy-start.3
  362.4 4.1 copy-start.2
  362.4 205.7 %all-to-all-start.1 = ((bf16[32,20,2,3584]{3,2,1,0:T(2,128)(2,1)}), bf16[32,20,2,3584]{3,2,1,0:T(2,128)(2,1)}, u32[]{:S(2)}, u32[]{:S(2)}) async-start(bf16[32,20,2,3584]{3,2,1,0:T(2,128)(2,1)} %copy.30), calls=%async_computation.1 | async-start | bytes 18350080 | tf_op jit(solution)/shard_map/all_to_all | solution.py:62
  568.2 56.2 %slice-start = ((s8[7340032]{0:T(1024)(128)(4,1)}), s8[3145728]{0:T(1024)(128)(4,1)S(1)}, s32[]{:S(2)}) async-start(s8[7340032]{0:T(1024)(128)(4,1)} %bitcast.80), calls=%async_computation.2 | async-start | bytes 6291456
  597.6 26.8 %slice-start.1 = ((s8[7340032]{0:T(1024)(128)(4,1)}), s8[4194304]{0:T(1024)(128)(4,1)S(1)}, s32[]{:S(2)}) async-start(s8[7340032]{0:T(1024)(128)(4,1)} %bitcast.80), calls=%async_computation.3 | async-start | bytes 8388608
  613.0 11.3 %copy-start = (bf16[512,2,3584]{2,1,0:T(2,128)(2,1)S(1)}, bf16[512,2,3584]{2,1,0:T(2,128)(2,1)}, u32[]{:S(2)}) copy-start(bf16[512,2,3584]{2,1,0:T(2,128)(2,1)} %gather_fusion.1) | copy-start | bytes 22020100
where the time goes:
time: 664 us; the launch traced here: 656 us
  blocking collectives  209 us (31%)
  waiting for transfers between devices  186 us (28%)
  local copies, waits for them, and re-layouts  139 us (21%)
  matrix products  77.7 us (12%)
  other arithmetic  38.3 us (6%)
    all_to_all x1, blocking collectives, per_device(): lax.all_to_all(send_rows.reshape(owners, capacity, 2, features), ('cp', '...  209 us
    all_to_all x1, waiting for transfers between devices, per_device(): lax.all_to_all(outcome.reshape(received.shape), ('cp', 'ep'), split_axis=...  186 us
    gather x1, local copies, waits for them, and re-layouts, per_device(): send_rows = stacked[slot_token]  31.5 us
    gather x1, local copies, waits for them, and re-layouts, per_device(): fetched = returned.reshape(owners * capacity, 2, features)[dest_slot]  29.4 us
    reduce_sum x1, other arithmetic, per_device(): jnp.sum(cotangent[0].astype(jnp.float32)[:, None, :] * expert_out, axis=-1)  27.7 us
    another operation x3, local copies, waits for them, and re-layouts, expert_rows(): return jnp.stack([expert_out, expert_grad], 1)  22.9 us
    dot_general x1, matrix products, expert_rows(): jnp.dot(grad_gate, gate_matrix.T, preferred_element_type=jnp.float32)  15.7 us
    mul x2, local copies, waits for them, and re-layouts, per_device(): cotangent[0].astype(jnp.float32)[:, None, :] * expert_out  15.6 us
  transfers between devices with their start and end apart: 1, of which 1 were waited for; matrix products, arithmetic and copies ran while one was open for 2% of the time, Pallas kernels for 0%

commit v1 on v0

v1 whole, which is shorter than its diff:
```python
import jax
import jax.numpy as jnp
from jax import lax
from jax.sharding import PartitionSpec as P

F32 = jnp.float32
BF16 = jnp.bfloat16


def dot(a, b, contract=(1, 0)):
    return lax.dot_general(
        a, b, (((contract[0],), (contract[1],)), ((), ())), preferred_element_type=F32
    )


def per_device(tokens, cotangent, routes, router_weights, w_gate, w_up, w_down):
    cp_count = lax.axis_size("cp")
    ep_count = lax.axis_size("ep")
    owners = cp_count * ep_count
    positions = tokens.shape[1]
    features = tokens.shape[2]
    top_k = routes.shape[2]
    capacity = positions * top_k // owners * 5 // 4
    part = ep_count * capacity
    everyone = ep_count * positions
    my_cp = lax.axis_index("cp")
    my_ep = lax.axis_index("ep")
    gate_matrix = w_gate[0]
    up_matrix = w_up[0]
    down_matrix = w_down[0]

    meta = jnp.concatenate([routes[0].astype(F32), router_weights[0]], axis=1)
    meta = lax.all_gather(meta, "ep", axis=0, tiled=False)
    tok_all = lax.all_gather(tokens[0], "ep", axis=0, tiled=True)
    cot_all = lax.all_gather(cotangent[0], "ep", axis=0, tiled=True)

    def partner(step):
        return lax.rem(my_cp + step, cp_count)

    def out_to(step, value):
        return lax.ppermute(value, "cp", [(c, (c + step) % cp_count) for c in range(cp_count)])

    def back_from(step, value):
        return lax.ppermute(value, "cp", [((c + step) % cp_count, c) for c in range(cp_count)])

    all_routes = meta[:, :, :top_k].astype(jnp.int32)
    all_weights = meta[:, :, top_k:]
    earlier = (jnp.arange(positions)[:, None] < jnp.arange(positions)[None, :]).astype(F32)
    names, slots, weights = [], [], []
    for step in range(cp_count):
        expert = partner(step) * ep_count + my_ep
        named = all_routes == expert
        named_any = jnp.any(named, axis=2)
        rank = dot(named_any.astype(F32), earlier).astype(jnp.int32)
        base = jnp.arange(ep_count, dtype=jnp.int32)[:, None] * capacity
        slots.append(jnp.where(named_any, base + rank, -1).reshape(1, everyone))
        weights.append(jnp.sum(jnp.where(named, all_weights, 0.0), axis=2).reshape(everyone, 1))
        names.append(named)
    row_ids = jnp.arange(part, dtype=jnp.int32)
    pick = [row_ids[:, None] == slot for slot in slots]

    def dispatch(dense):
        packed = [dot(p.astype(BF16), dense).astype(BF16) for p in pick]
        arrived = [packed[0]] + [out_to(s, packed[s]) for s in range(1, cp_count)]
        return packed, jnp.concatenate(arrived, axis=0)

    _, inputs = dispatch(tok_all)
    cot_packed, grad_in = dispatch(cot_all)

    gate_pre = dot(inputs, gate_matrix)
    up_pre = dot(inputs, up_matrix)
    sig_gate = jax.nn.sigmoid(gate_pre)
    silu_gate = gate_pre * sig_gate
    hidden = (silu_gate * up_pre).astype(BF16)
    expert_out = dot(hidden, down_matrix).astype(BF16)

    spread = []
    for step in range(cp_count):
        here = row_ids[None, :] == slots[step].reshape(everyone, 1)
        spread.append(jnp.where(here, weights[step], 0.0))
    spread = jnp.concatenate(spread, axis=1)
    spread_hi = lax.reduce_precision(spread, 8, 7)
    spread_lo = (spread - spread_hi).astype(BF16)
    spread_hi = spread_hi.astype(BF16)

    def bring_back(rows):
        pieces = [rows[s * part:(s + 1) * part] for s in range(cp_count)]
        return [pieces[0]] + [back_from(s, pieces[s]) for s in range(1, cp_count)]

    def combine(pieces):
        rows = jnp.concatenate(pieces, axis=0)
        dense = (dot(spread_hi, rows) + dot(spread_lo, rows)).astype(BF16)
        return lax.psum_scatter(dense, "ep", scatter_dimension=0, tiled=True)

    out_pieces = bring_back(expert_out)

    grad_hidden = dot(grad_in, down_matrix, (1, 1))
    grad_gate = (grad_hidden * up_pre * sig_gate * (1.0 + gate_pre * (1.0 - sig_gate))).astype(BF16)
    grad_up = (grad_hidden * silu_gate).astype(BF16)
    expert_grad = (
        dot(grad_gate, gate_matrix, (1, 1)) + dot(grad_up, up_matrix, (1, 1))
    ).astype(BF16)
    grad_pieces = bring_back(expert_grad)

    layer_out = combine(out_pieces)
    gate_parts = jnp.zeros((ep_count, positions, top_k), F32)
    for step in range(cp_count):
        scores = jnp.sum(
            cot_packed[step].astype(F32) * out_pieces[step].astype(F32), axis=1, keepdims=True
        )
        by_token = jnp.sum(jnp.where(pick[step], scores, 0.0), axis=0)
        gate_parts += jnp.where(names[step], by_token.reshape(ep_count, positions, 1), 0.0)
    gate_grad = lax.psum_scatter(gate_parts, "ep", scatter_dimension=0, tiled=False)
    token_grad = combine(grad_pieces)
    return layer_out[None], token_grad[None], gate_grad[None]


def solution(mesh):
    in_specs = (
        P("ep", "cp", None),
        P("ep", "cp", None),
        P("ep", "cp", None),
        P("ep", "cp", None),
        P(("cp", "ep"), None, None),
        P(("cp", "ep"), None, None),
        P(("cp", "ep"), None, None),
    )
    out_specs = (P("ep", "cp", None), P("ep", "cp", None), P("ep", "cp", None))
    return jax.shard_map(
        per_device, mesh=mesh, in_specs=in_specs, out_specs=out_specs, check_vma=False
    )
```

time: 664 us -> 386 us (0.58); the launches traced: 656 us -> 385 us
  blocking collectives: 209 us -> 43.3 us
  local copies, waits for them, and re-layouts: 139 us -> 16.5 us
  starting transfers between devices: 3.99 us -> 41.3 us
  other arithmetic: 38.3 us -> 5.37 us
  matrix products: 77.7 us -> 102 us
  waiting for transfers between devices: 186 us -> 163 us
  between operations: 1.01 us -> 14.1 us
    all_to_all x1 -> x0, blocking collectives: 209 us -> none  [per_device(): lax.all_to_all(send_rows.reshape(owners, capacity, 2, features), ('cp', '...]
    all_to_all x1 -> x0, waiting for transfers between devices: 186 us -> none  [per_device(): lax.all_to_all(outcome.reshape(received.shape), ('cp', 'ep'), split_axis=...]
    ppermute x0 -> x12, waiting for transfers between devices: none -> 118 us  [the longest x6 69.4 us: back_from(): lax.ppermute(value, 'cp', [((c + step) % cp_count, c) for c in range(cp_c...]
    gather x2 -> x0, local copies, waits for them, and re-layouts: 60.9 us -> none  [the longest x1 31.5 us: per_device(): send_rows = stacked[slot_token]]
    ppermute x0 -> x12, starting transfers between devices: none -> 41 us  [the longest x6 32.6 us: out_to(): lax.ppermute(value, 'cp', [(c, (c + step) % cp_count) for c in range(cp_c...]
    all_gather x0 -> x2, waiting for transfers between devices: none -> 28.8 us  [the longest x1 28.8 us: per_device(): tok_all = lax.all_gather(tokens[0], 'ep', axis=0, tiled=True)]
    unnamed x0 -> x1, blocking collectives: none -> 27.5 us
    another operation x6 -> x0, local copies, waits for them, and re-layouts: 26.4 us -> none  [the longest x3 22.9 us: expert_rows(): return jnp.stack([expert_out, expert_grad], 1)]
  transfers between devices with their start and end apart: 1 -> 16, of which waited for: 1 -> 10; matrix products, arithmetic and copies ran while one was open for 2% -> 30% of each run, Pallas kernels for 0% -> 0%
where the time goes in v1:
time: 386 us; the launch traced here: 385 us
  waiting for transfers between devices  163 us (42%)
  matrix products  102 us (26%)
  blocking collectives  43.3 us (11%)
  starting transfers between devices  41.3 us (11%)
  local copies, waits for them, and re-layouts  16.5 us (4%)
  between operations  14.1 us (4%)
  other arithmetic  5.37 us (1%)
    dot_general x22, matrix products, dot(): lax.dot_general(a, b, (((contract[0],), (contract[1],)), ((), ())), prefe...  102 us
    ppermute x6, waiting for transfers between devices, back_from(): lax.ppermute(value, 'cp', [((c + step) % cp_count, c) for c in range(cp_c...  69.4 us
    ppermute x6, waiting for transfers between devices, out_to(): lax.ppermute(value, 'cp', [(c, (c + step) % cp_count) for c in range(cp_c...  49.1 us
    ppermute x6, starting transfers between devices, out_to(): lax.ppermute(value, 'cp', [(c, (c + step) % cp_count) for c in range(cp_c...  32.6 us
    all_gather x1, waiting for transfers between devices, per_device(): tok_all = lax.all_gather(tokens[0], 'ep', axis=0, tiled=True)  28.8 us
    unnamed x1, blocking collectives  27.5 us
    all_gather x1, blocking collectives, per_device(): meta = lax.all_gather(meta, 'ep', axis=0, tiled=False)  15.7 us
    reduce_scatter x2, waiting for transfers between devices, combine(): return lax.psum_scatter(dense, 'ep', scatter_dimension=0, tiled=True)  14.6 us
  transfers between devices with their start and end apart: 16, of which 10 were waited for; matrix products, arithmetic and copies ran while one was open for 30% of the time, Pallas kernels for 0%

profile of v1, /device:TPU:0, one launch (start us, length us, event | category | flops | bytes accessed | tf_op | source)
XLA Modules:
  0.0 385.3 jit_solution(5477556809834293592)
XLA Ops:
  8.0 0.7 convert_bitcast_fusion
  9.3 15.7 %all-gather.3 = f32[8,64,16]{1,2,0:T(8,128)S(1)} all-gather(f32[1,64,16]{1,2,0:T(8,128)S(1)} %maximum_bitcast_fusion), channel_id=2, replica_groups=mesh['cp'=4,'ep'=8] {'ep'}, dimensions={0}, use_global_device_ids=true | all-gather | bytes 36864 | tf_op jit(solution)/shard_map/all_gather | solution.py:33
  26.3 28.8 %all-gather.7.cloned.1.call-done = bf16[1,512,3584]{2,1,0:T(8,128)(2,1)} async-done(((bf16[1,64,3584]{2,1,0:T(8,128)(2,1)}), bf16[1,512,3584]{2,1,0:T(8,128)(2,1)}) %all-gather.7.cloned.1.call-update) | async-done | bytes 3670032 | tf_op jit(solution)/shard_map/all_gather | solution.py:34
  55.1 3.0 convolution_convert_fusion.4
  58.0 2.4 collective-permute-start.2
  60.4 0.8 convolution_convert_fusion.6
  61.3 0.8 convolution_convert_fusion.5
  62.1 1.2 collective-permute-start.1
  63.7 3.0 convolution_convert_fusion.7
  66.7 19.5 %collective-permute-done.2 = bf16[160,3584]{1,0:T(8,128)(2,1)} collective-permute-done((bf16[160,3584]{1,0:T(8,128)(2,1)S(1)}, bf16[160,3584]{1,0:T(8,128)(2,1)}, u32[]{:S(2)}, u32[]{:S(2)}) %collective-permute-start.2) | collective-permute-done | bytes 1146912 | tf_op jit(solution)/shard_map/ppermute | solution.py:41
  86.3 24.9 %collective-permute-done = bf16[160,3584]{1,0:T(8,128)(2,1)} collective-permute-done((bf16[160,3584]{1,0:T(8,128)(2,1)S(1)}, bf16[160,3584]{1,0:T(8,128)(2,1)}, u32[]{:S(2)}, u32[]{:S(2)}) %collective-permute-start) | collective-permute-done | bytes 1146912 | tf_op jit(solution)/shard_map/ppermute | solution.py:41
  111.2 2.8 collective-permute-done.1
  114.0 9.7 %fusion.10 = f32[640,1024]{1,0:T(8,128)S(1)} fusion(bf16[1,3584,1024]{2,1,0:T(8,128)(2,1)} %param.11, bf16[160,3584]{1,0:T(8,128)(2,1)} %collective-permute-done.2, bf16[160,3584]{1,0:T(8,128)(2,1)} %collective-permute-done.1, bf16[160,3584]{1,0:T(8,128)(2,1)} %collective-permute-done, bf16[160,3584]{1,0:T(8,128)(2,1)S(1)} %convolution_convert_fusion.7), kind=kOutput, calls=%fused_computation.11 | convolution fusion | flops 4715970560 | bytes 14548992 | tf_op jit(solution)/shard_map/dot_general | solution.py:11
  123.7 8.6 %fusion.6 = f32[640,1024]{1,0:T(8,128)S(1)} fusion(bf16[1,3584,1024]{2,1,0:T(8,128)(2,1)S(1)} %bitcast.65, bf16[160,3584]{1,0:T(8,128)(2,1)} %collective-permute-done.2, bf16[160,3584]{1,0:T(8,128)(2,1)} %collective-permute-done.1, bf16[160,3584]{1,0:T(8,128)(2,1)} %collective-permute-done, bf16[160,3584]{1,0:T(8,128)(2,1)S(1)} %convolution_convert_fusion.7), kind=kOutput, calls=%fused_computation.7 | convolution fusion | flops 4715970560 | bytes 14548992 | tf_op jit(solution)/shard_map/dot_general | solution.py:11
  132.4 1.5 copy-done.12
  133.9 5.9 %fusion.12 = bf16[640,3584]{1,0:T(8,128)(2,1)S(1)} fusion(bf16[1,1024,3584]{2,1,0:T(8,128)(2,1)S(1)} %bitcast.63, f32[640,1024]{1,0:T(8,128)S(1)} %fusion.6, f32[640,1024]{1,0:T(8,128)S(1)} %fusion.10), kind=kOutput, calls=%fused_computation.15 | convolution fusion | flops 4703846400 | bytes 17170432 | tf_op jit(solution)/shard_map/dot_general | solution.py:11
  139.8 1.9 fusion.82
  142.2 0.8 collective-permute-start.4
  143.0 2.9 collective-permute-start.3
  146.0 4.2 %multiply_reduce_fusion.3 = (f32[160]{0:T(256)S(1)}, bf16[160,3584]{1,0:T(8,128)(2,1)}) fusion(bf16[640,3584]{1,0:T(8,128)(2,1)} %copy-done.1, bf16[1,512,3584]{2,1,0:T(8,128)(2,1)} %all-gather.9.cloned.1.call-done, s32[512]{0:T(512)S(1)} %eq.139), kind=kOutput, calls=%fused_computation.50 | convolution fusion | flops 590151552 | bytes 5966464 | tf_op jit(solution)/shard_map/dot_general | solution.py:11
  150.9 20.7 %collective-permute-done.5 = bf16[160,3584]{1,0:T(8,128)(2,1)} collective-permute-done((bf16[160,3584]{1,0:T(8,128)(2,1)}, bf16[160,3584]{1,0:T(8,128)(2,1)}, u32[]{:S(2)}, u32[]{:S(2)}) %collective-permute-start.5) | collective-permute-done | bytes 1146912 | tf_op jit(solution)/shard_map/ppermute | solution.py:44
  171.6 4.2 %multiply_reduce_fusion = (f32[160]{0:T(256)S(1)}, bf16[160,3584]{1,0:T(8,128)(2,1)}) fusion(bf16[160,3584]{1,0:T(8,128)(2,1)} %collective-permute-done.5, bf16[1,512,3584]{2,1,0:T(8,128)(2,1)} %all-gather.9.cloned.1.call-done, s32[512]{0:T(512)S(1)} %eq.157), kind=kOutput, calls=%fused_computation.47 | convolution fusion | flops 590151552 | bytes 5966464 | tf_op jit(solution)/shard_map/dot_general | solution.py:11
  176.6 16.6 %collective-permute-done.4 = bf16[160,3584]{1,0:T(8,128)(2,1)} collective-permute-done((bf16[160,3584]{1,0:T(8,128)(2,1)S(1)}, bf16[160,3584]{1,0:T(8,128)(2,1)}, u32[]{:S(2)}, u32[]{:S(2)}) %collective-permute-start.4) | collective-permute-done | bytes 1146912 | tf_op jit(solution)/shard_map/ppermute | solution.py:44
  193.2 3.2 multiply_reduce_fusion.1
  197.8 3.2 multiply_reduce_fusion.2
  201.9 1.4 select_reduce_fusion.7
  203.3 0.7 broadcast_in_dim.144
  204.1 0.7 broadcast_in_dim.147
  204.8 0.8 broadcast_in_dim.149
  205.6 0.8 broadcast_in_dim.151
  207.2 28.3 %collective-permute-start.6 = (bf16[160,3584]{1,0:T(8,128)(2,1)S(1)}, bf16[160,3584]{1,0:T(8,128)(2,1)}, u32[]{:S(2)}, u32[]{:S(2)}) collective-permute-start(bf16[160,3584]{1,0:T(8,128)(2,1)S(1)} %get-tuple-element.37), channel_id=1, source_target_pairs={{0,8},{8,16},{16,24},{24,0},{1,9},{9,17},{17,25},{25,1},{2,10},{10... | collective-permute-start | bytes 3440648 | tf_op jit(solution)/shard_map/ppermute | solution.py:41
  236.1 5.2 %fusion.44 = f32[512,3584]{1,0:T(8,128)S(1)} fusion(bf16[512,640]{1,0:T(8,128)(2,1)S(1)} %get-tuple-element.24, bf16[160,3584]{1,0:T(8,128)(2,1)} %collective-permute-done.5, bf16[160,3584]{1,0:T(8,128)(2,1)} %collective-permute-done.4, bf16[160,3584]{1,0:T(8,128)(2,1)} %collective-permute-done.3, bf16[160,3584]{1,0:T(8,128)(2,1)S(1)} %get-tuple-element.19), kind=kOutput, calls=%fused_computation.69 | convolution fusion | flops 2367160320 | bytes 12582912 | tf_op jit(solution)/shard_map/dot_general | solution.py:11
  241.3 5.9 %add_convert_fusion.2 = bf16[512,3584]{1,0:T(8,128)(2,1)} fusion(f32[512,3584]{1,0:T(8,128)S(1)} %fusion.44, bf16[512,640]{1,0:T(8,128)(2,1)S(1)} %get-tuple-element.23, bf16[160,3584]{1,0:T(8,128)(2,1)} %collective-permute-done.5, bf16[160,3584]{1,0:T(8,128)(2,1)} %collective-permute-done.4, bf16[160,3584]{1,0:T(8,128)(2,1)} %collective-permute-done.3, ...), kind=kOutput, calls=%fused_computation.14 | convolution fusion | flops 2370830336 | bytes 16252928 | tf_op jit(solution)/shard_map/dot_general | solution.py:11
  247.3 1.8 collective-permute-done.6
  249.2 10.2 %fusion = f32[640,1024]{1,0:T(8,128)S(1)} fusion(bf16[1,1024,3584]{2,1,0:T(8,128)(2,1)} %param.13, bf16[160,3584]{1,0:T(8,128)(2,1)} %collective-permute-done.8, bf16[160,3584]{1,0:T(8,128)(2,1)} %collective-permute-done.7, bf16[160,3584]{1,0:T(8,128)(2,1)} %collective-permute-done.6, bf16[160,3584]{1,0:T(8,128)(2,1)S(1)} %copy-done.2), kind=kOutput, calls=%fused_computation.1 | convolution fusion | flops 4715970560 | bytes 14548992 | tf_op jit(solution)/shard_map/dot_general | solution.py:11
  259.4 1.5 copy-done.11
  260.9 10.7 %fusion.4 = f32[640,3584]{1,0:T(8,128)} fusion(bf16[1,3584,1024]{2,1,0:T(8,128)(2,1)} %param.12, f32[640,1024]{1,0:T(8,128)S(1)} %fusion, f32[640,1024]{1,0:T(8,128)S(1)} %copy-done.9), kind=kOutput, calls=%fused_computation.5 | convolution fusion | flops 4701552640 | bytes 21757952 | tf_op jit(solution)/shard_map/dot_general | solution.py:11
  271.6 15.3 %add_convert_fusion = bf16[640,3584]{1,0:T(8,128)(2,1)} fusion(f32[640,3584]{1,0:T(8,128)} %fusion.4, bf16[1,3584,1024]{2,1,0:T(8,128)(2,1)} %param.11, f32[640,1024]{1,0:T(8,128)S(1)} %copy-done.10, f32[640,1024]{1,0:T(8,128)} %copy-done.11, f32[640,1024]{1,0:T(8,128)} %copy-done.12), kind=kOutput, calls=%fused_computation | convolution fusion | flops 4708761600 | bytes 28966912 | tf_op jit(solution)/shard_map/dot_general | solution.py:11
  286.9 2.7 fusion.81
  289.6 2.2 collective-permute-start.11
  292.3 2.0 collective-permute-start.9
  294.3 19.9 %collective-permute-done.11 = bf16[160,3584]{1,0:T(8,128)(2,1)S(1)} collective-permute-done((bf16[160,3584]{1,0:T(8,128)(2,1)S(1)}, bf16[160,3584]{1,0:T(8,128)(2,1)S(1)}, u32[]{:S(2)}, u32[]{:S(2)}) %collective-permute-start.11) | collective-permute-done | bytes 1146912 | tf_op jit(solution)/shard_map/ppermute | solution.py:44
  314.2 12.1 %collective-permute-done.10 = bf16[160,3584]{1,0:T(8,128)(2,1)S(1)} collective-permute-done((bf16[160,3584]{1,0:T(8,128)(2,1)S(1)}, bf16[160,3584]{1,0:T(8,128)(2,1)S(1)}, u32[]{:S(2)}, u32[]{:S(2)}) %collective-permute-start.10) | collective-permute-done | bytes 1146912 | tf_op jit(solution)/shard_map/ppermute | solution.py:44
  326.4 3.2 fusion.43
  329.6 4.6 %add_convert_fusion.1 = bf16[512,3584]{1,0:T(8,128)(2,1)} fusion(f32[512,3584]{1,0:T(8,128)S(1)} %fusion.43, bf16[512,640]{1,0:T(8,128)(2,1)S(1)} %copy-done.4, bf16[160,3584]{1,0:T(8,128)(2,1)S(1)} %collective-permute-done.11, bf16[160,3584]{1,0:T(8,128)(2,1)S(1)} %collective-permute-done.10, bf16[160,3584]{1,0:T(8,128)(2,1)S(1)} %collective-permute-done.9, ...), kind=kOutput, calls=%fused_computation.13 | convolution fusion | flops 2370830336 | bytes 16252928 | tf_op jit(solution)/shard_map/dot_general | solution.py:11
  335.5 27.5 %all-reduce = f32[8,64,8]{1,2,0:T(8,128)S(1)} all-reduce(f32[8,64,8]{1,2,0:T(8,128)S(1)} %get-tuple-element.31), channel_id=7, replica_groups=mesh['cp'=4,'ep'=8] {'ep'}, use_global_device_ids=true, to_apply=%region_18.19.clone | all-reduce | flops 4096 | bytes 32768
  363.0 1.2 constant_dynamic-slice_fusion
  364.2 14.6 %reduce-scatter.5.cloned.1.call-done = bf16[64,3584]{1,0:T(8,128)(2,1)} async-done(((bf16[512,3584]{1,0:T(8,128)(2,1)}), bf16[64,3584]{1,0:T(8,128)(2,1)}) %reduce-scatter.5.cloned.1.call-update) | async-done | bytes 458768 | tf_op jit(solution)/shard_map/reduce_scatter | solution.py:93
  (78 shorter events, 10.7 us)
Async XLA Ops:
  7.2 47.9 %all-gather.7.cloned.1.call-start = ((), (), s32[]{:S(2)}) async-start(), calls=%async_computation.4 | async-start | bytes 4128768 | tf_op jit(solution)/shard_map/all_gather | solution.py:34
  7.9 138.1 %all-gather.9.cloned.1.call-start = ((), (), s32[]{:S(2)}) async-start(), calls=%async_computation.5 | async-start | bytes 4128768 | tf_op jit(solution)/shard_map/all_gather | solution.py:35
  55.1 5.4 %copy-start = (bf16[1,512,3584]{2,1,0:T(8,128)(2,1)S(1)}, bf16[1,512,3584]{2,1,0:T(8,128)(2,1)}, u32[]{:S(2)}) copy-start(bf16[1,512,3584]{2,1,0:T(8,128)(2,1)} %all-gather.7.cloned.1.call-done) | copy-start | bytes 11010052
  58.0 28.3 %collective-permute-start.2 = (bf16[160,3584]{1,0:T(8,128)(2,1)S(1)}, bf16[160,3584]{1,0:T(8,128)(2,1)}, u32[]{:S(2)}, u32[]{:S(2)}) collective-permute-start(bf16[160,3584]{1,0:T(8,128)(2,1)S(1)} %convolution_convert_fusion.4), channel_id=1, source_target_pairs={{0,24},{8,0},{16,8},{24,16},{1,25},{9,1},{17,9},{25,17},{2,26},{10... | collective-permute-start | bytes 3440648 | tf_op jit(solution)/shard_map/ppermute | solution.py:41
  61.2 49.9 %collective-permute-start = (bf16[160,3584]{1,0:T(8,128)(2,1)S(1)}, bf16[160,3584]{1,0:T(8,128)(2,1)}, u32[]{:S(2)}, u32[]{:S(2)}) collective-permute-start(bf16[160,3584]{1,0:T(8,128)(2,1)S(1)} %convolution_convert_fusion.6), channel_id=1, source_target_pairs={{0,8},{8,16},{16,24},{24,0},{1,9},{9,17},{17,25},{25,1},{2,10},{10... | collective-permute-start | bytes 3440648 | tf_op jit(solution)/shard_map/ppermute | solution.py:41
  62.1 51.9 %collective-permute-start.1 = (bf16[160,3584]{1,0:T(8,128)(2,1)S(1)}, bf16[160,3584]{1,0:T(8,128)(2,1)}, u32[]{:S(2)}, u32[]{:S(2)}) collective-permute-start(bf16[160,3584]{1,0:T(8,128)(2,1)S(1)} %convolution_convert_fusion.5), channel_id=1, source_target_pairs={{0,16},{8,24},{16,0},{24,8},{1,17},{9,25},{17,1},{25,9},{2,18},{10... | collective-permute-start | bytes 3440648 | tf_op jit(solution)/shard_map/ppermute | solution.py:41
  63.3 300.9 %reduce-scatter.3.cloned.1.call-start = ((), (), s32[]{:S(2)}) async-start(), calls=%async_computation.2 | async-start | bytes 4128768 | tf_op jit(solution)/shard_map/reduce_scatter | solution.py:93
  63.7 60.0 %slice-start.2 = ((s8[7340032]{0:T(1024)(128)(4,1)}), s8[4194304]{0:T(1024)(128)(4,1)S(1)}, s32[]{:S(2)}) async-start(s8[7340032]{0:T(1024)(128)(4,1)} %bitcast.64), calls=%async_computation.8 | async-start | bytes 8388608
  63.7 70.2 %slice-start = ((s8[7340032]{0:T(1024)(128)(4,1)}), s8[4194304]{0:T(1024)(128)(4,1)S(1)}, s32[]{:S(2)}) async-start(s8[7340032]{0:T(1024)(128)(4,1)} %bitcast.62), calls=%async_computation.6 | async-start | bytes 8388608
  66.7 57.0 %slice-start.3 = ((s8[7340032]{0:T(1024)(128)(4,1)}), s8[3145728]{0:T(1024)(128)(4,1)S(1)}, s32[]{:S(2)}) async-start(s8[7340032]{0:T(1024)(128)(4,1)} %bitcast.64), calls=%async_computation.9 | async-start | bytes 6291456
  66.7 67.1 %slice-start.1 = ((s8[7340032]{0:T(1024)(128)(4,1)}), s8[3145728]{0:T(1024)(128)(4,1)S(1)}, s32[]{:S(2)}) async-start(s8[7340032]{0:T(1024)(128)(4,1)} %bitcast.62), calls=%async_computation.7 | async-start | bytes 6291456
  123.7 8.6 %copy-start.8 = (f32[640,1024]{1,0:T(8,128)}, f32[640,1024]{1,0:T(8,128)S(1)}, u32[]{:S(2)}) copy-start(f32[640,1024]{1,0:T(8,128)S(1)} %fusion.10) | copy-start | bytes 7864324
  132.4 1.5 copy-start.12
  139.8 2.4 copy-start.1
  142.2 29.4 %collective-permute-start.5 = (bf16[160,3584]{1,0:T(8,128)(2,1)}, bf16[160,3584]{1,0:T(8,128)(2,1)}, u32[]{:S(2)}, u32[]{:S(2)}) collective-permute-start(bf16[160,3584]{1,0:T(8,128)(2,1)} %get-tuple-element.20), channel_id=1, source_target_pairs={{24,0},{0,8},{8,16},{16,24},{25,1},{1,9},{9,17},{17,25},{26,2},{2,... | collective-permute-start | bytes 3440648 | tf_op jit(solution)/shard_map/ppermute | solution.py:44
  142.2 51.0 %collective-permute-start.4 = (bf16[160,3584]{1,0:T(8,128)(2,1)S(1)}, bf16[160,3584]{1,0:T(8,128)(2,1)}, u32[]{:S(2)}, u32[]{:S(2)}) collective-permute-start(bf16[160,3584]{1,0:T(8,128)(2,1)S(1)} %get-tuple-element.21), channel_id=1, source_target_pairs={{16,0},{24,8},{0,16},{8,24},{17,1},{25,9},{1,17},{9,25},{18,2},{26... | collective-permute-start | bytes 3440648 | tf_op jit(solution)/shard_map/ppermute | solution.py:44
  143.0 54.8 %collective-permute-start.3 = (bf16[160,3584]{1,0:T(8,128)(2,1)S(1)}, bf16[160,3584]{1,0:T(8,128)(2,1)}, u32[]{:S(2)}, u32[]{:S(2)}) collective-permute-start(bf16[160,3584]{1,0:T(8,128)(2,1)S(1)} %get-tuple-element.22), channel_id=1, source_target_pairs={{8,0},{16,8},{24,16},{0,24},{9,1},{17,9},{25,17},{1,25},{10,2},{18... | collective-permute-start | bytes 3440648 | tf_op jit(solution)/shard_map/ppermute | solution.py:44
  176.6 70.7 %collective-permute-start.8 = (bf16[160,3584]{1,0:T(8,128)(2,1)}, bf16[160,3584]{1,0:T(8,128)(2,1)}, u32[]{:S(2)}, u32[]{:S(2)}) collective-permute-start(bf16[160,3584]{1,0:T(8,128)(2,1)} %get-tuple-element.33), channel_id=1, source_target_pairs={{0,24},{8,0},{16,8},{24,16},{1,25},{9,1},{17,9},{25,17},{2,26},{10... | collective-permute-start | bytes 3440648 | tf_op jit(solution)/shard_map/ppermute | solution.py:41
  197.2 50.1 %collective-permute-start.7 = (bf16[160,3584]{1,0:T(8,128)(2,1)S(1)}, bf16[160,3584]{1,0:T(8,128)(2,1)}, u32[]{:S(2)}, u32[]{:S(2)}) collective-permute-start(bf16[160,3584]{1,0:T(8,128)(2,1)S(1)} %get-tuple-element.35), channel_id=1, source_target_pairs={{0,16},{8,24},{16,0},{24,8},{1,17},{9,25},{17,1},{25,9},{2,18},{10... | collective-permute-start | bytes 3440648 | tf_op jit(solution)/shard_map/ppermute | solution.py:41
  207.2 42.0 %collective-permute-start.6 = (bf16[160,3584]{1,0:T(8,128)(2,1)S(1)}, bf16[160,3584]{1,0:T(8,128)(2,1)}, u32[]{:S(2)}, u32[]{:S(2)}) collective-permute-start(bf16[160,3584]{1,0:T(8,128)(2,1)S(1)} %get-tuple-element.37), channel_id=1, source_target_pairs={{0,8},{8,16},{16,24},{24,0},{1,9},{9,17},{17,25},{25,1},{2,10},{10... | collective-permute-start | bytes 3440648 | tf_op jit(solution)/shard_map/ppermute | solution.py:41
  236.1 5.2 %copy-start.5 = (bf16[512,640]{1,0:T(8,128)(2,1)}, bf16[512,640]{1,0:T(8,128)(2,1)S(1)}, u32[]{:S(2)}) copy-start(bf16[512,640]{1,0:T(8,128)(2,1)S(1)} %get-tuple-element.24) | copy-start | bytes 1966084
  236.1 5.2 %copy-start.3 = (bf16[512,640]{1,0:T(8,128)(2,1)}, bf16[512,640]{1,0:T(8,128)(2,1)S(1)}, u32[]{:S(2)}) copy-start(bf16[512,640]{1,0:T(8,128)(2,1)S(1)} %get-tuple-element.23) | copy-start | bytes 1966084
  247.2 1.9 copy-start.2
  247.2 131.5 %reduce-scatter.5.cloned.1.call-start = ((), (), s32[]{:S(2)}) async-start(), calls=%async_computation.3 | async-start | bytes 4128768 | tf_op jit(solution)/shard_map/reduce_scatter | solution.py:93
  249.2 11.7 %copy-start.9 = (f32[640,1024]{1,0:T(8,128)S(1)}, f32[640,1024]{1,0:T(8,128)}, u32[]{:S(2)}) copy-start(f32[640,1024]{1,0:T(8,128)} %copy-done.8) | copy-start | bytes 7864324
  259.4 1.5 copy-start.11
  260.9 10.7 %copy-start.10 = (f32[640,1024]{1,0:T(8,128)S(1)}, f32[640,1024]{1,0:T(8,128)}, u32[]{:S(2)}) copy-start(f32[640,1024]{1,0:T(8,128)} %copy-done.8) | copy-start | bytes 7864324
  286.9 39.5 %copy-start.6 = (bf16[512,640]{1,0:T(8,128)(2,1)S(1)}, bf16[512,640]{1,0:T(8,128)(2,1)}, u32[]{:S(2)}) copy-start(bf16[512,640]{1,0:T(8,128)(2,1)} %copy-done.5) | copy-start | bytes 1966084
  289.6 24.6 %collective-permute-start.11 = (bf16[160,3584]{1,0:T(8,128)(2,1)S(1)}, bf16[160,3584]{1,0:T(8,128)(2,1)S(1)}, u32[]{:S(2)}, u32[]{:S(2)}) collective-permute-start(bf16[160,3584]{1,0:T(8,128)(2,1)S(1)} %get-tuple-element.16), channel_id=1, source_target_pairs={{24,0},{0,8},{8,16},{16,24},{25,1},{1,9},{9,17},{17,25},{26,2},{2,... | collective-permute-start | bytes 3440648 | tf_op jit(solution)/shard_map/ppermute | solution.py:44
  291.7 34.6 %collective-permute-start.10 = (bf16[160,3584]{1,0:T(8,128)(2,1)S(1)}, bf16[160,3584]{1,0:T(8,128)(2,1)S(1)}, u32[]{:S(2)}, u32[]{:S(2)}) collective-permute-start(bf16[160,3584]{1,0:T(8,128)(2,1)S(1)} %get-tuple-element.17), channel_id=1, source_target_pairs={{16,0},{24,8},{0,16},{8,24},{17,1},{25,9},{1,17},{9,25},{18,2},{26... | collective-permute-start | bytes 3440648 | tf_op jit(solution)/shard_map/ppermute | solution.py:44
  292.3 34.1 %collective-permute-start.9 = (bf16[160,3584]{1,0:T(8,128)(2,1)S(1)}, bf16[160,3584]{1,0:T(8,128)(2,1)S(1)}, u32[]{:S(2)}, u32[]{:S(2)}) collective-permute-start(bf16[160,3584]{1,0:T(8,128)(2,1)S(1)} %get-tuple-element.18), channel_id=1, source_target_pairs={{8,0},{16,8},{24,16},{0,24},{9,1},{17,9},{25,17},{1,25},{10,2},{18... | collective-permute-start | bytes 3440648 | tf_op jit(solution)/shard_map/ppermute | solution.py:44
  326.4 3.3 copy-start.4
  334.3 0.7 copy-start.7
Sparse Core Ops, SparseCore 0:
  9.6 45.3 all-gather.6
  63.4 41.3 all-gather.8
  247.4 42.0 reduce-scatter.2
  334.4 44.2 reduce-scatter.4

commit v2 on v1

--- a/solution.py
+++ b/solution.py
@@ -59,13 +59,16 @@
     row_ids = jnp.arange(part, dtype=jnp.int32)
     pick = [row_ids[:, None] == slot for slot in slots]
 
-    def dispatch(dense):
-        packed = [dot(p.astype(BF16), dense).astype(BF16) for p in pick]
-        arrived = [packed[0]] + [out_to(s, packed[s]) for s in range(1, cp_count)]
-        return packed, jnp.concatenate(arrived, axis=0)
+    def pack(dense):
+        return [dot(p.astype(BF16), dense).astype(BF16) for p in pick]
 
-    _, inputs = dispatch(tok_all)
-    cot_packed, grad_in = dispatch(cot_all)
+    def dispatch(packed):
+        return [packed[0]] + [out_to(s, packed[s]) for s in range(1, cp_count)]
+
+    arrived = dispatch(pack(tok_all))
+    arrived, cot_packed = lax.optimization_barrier((arrived, pack(cot_all)))
+    inputs = jnp.concatenate(arrived, axis=0)
+    grad_in = jnp.concatenate(dispatch(cot_packed), axis=0)
 
     gate_pre = dot(inputs, gate_matrix)
     up_pre = dot(inputs, up_matrix)

time: 386 us -> 392 us (1.016)
  waiting for transfers between devices: 163 us -> 203 us
  starting transfers between devices: 41.3 us -> 13.1 us
  matrix products: 102 us -> 86 us
  other arithmetic: 5.37 us -> 10.4 us
  local copies, waits for them, and re-layouts: 16.5 us -> 21.4 us
    ppermute x6, waiting for transfers between devices: 69.4 us -> 116 us  [back_from(): lax.ppermute(value, 'cp', [((c + step) % cp_count, c) for c in range(cp_c...]
    ppermute x6, waiting for transfers between devices: 49.1 us -> 12.1 us  [out_to(): lax.ppermute(value, 'cp', [(c, (c + step) % cp_count) for c in range(cp_c...]
    all_gather x1, waiting for transfers between devices: 0.01 us -> 31.1 us  [per_device(): cot_all = lax.all_gather(cotangent[0], 'ep', axis=0, tiled=True)]
    ppermute x6, starting transfers between devices: 32.6 us -> 4.7 us  [out_to(): lax.ppermute(value, 'cp', [(c, (c + step) % cp_count) for c in range(cp_c...]
    dot_general x22, matrix products: 102 us -> 86 us  [dot(): lax.dot_general(a, b, (((contract[0],), (contract[1],)), ((), ())), prefe...]
    reduce_sum x0 -> x2, other arithmetic: none -> 5.03 us  [per_device(): jnp.sum(cot_packed[step].astype(F32) * out_pieces[step].astype(F32), axis...]
    unnamed x36 -> x51, local copies, waits for them, and re-layouts: 5.96 us -> 9.7 us
  transfers between devices with their start and end apart: 16 -> 16, of which waited for: 10 -> 11; matrix products, arithmetic and copies ran while one was open for 30% -> 23% of each run, Pallas kernels for 0% -> 0%
where the time goes in v2:
time: 392 us; the launch traced here: 391 us
  waiting for transfers between devices  203 us (52%)
  matrix products  86 us (22%)
  blocking collectives  43.2 us (11%)
  local copies, waits for them, and re-layouts  21.4 us (5%)
  between operations  14.2 us (4%)
  starting transfers between devices  13.1 us (3%)
  other arithmetic  10.4 us (3%)
    ppermute x6, waiting for transfers between devices, back_from(): lax.ppermute(value, 'cp', [((c + step) % cp_count, c) for c in range(cp_c...  116 us
    dot_general x22, matrix products, dot(): lax.dot_general(a, b, (((contract[0],), (contract[1],)), ((), ())), prefe...  86 us
    all_gather x1, waiting for transfers between devices, per_device(): cot_all = lax.all_gather(cotangent[0], 'ep', axis=0, tiled=True)  31.1 us
    all_gather x1, waiting for transfers between devices, per_device(): tok_all = lax.all_gather(tokens[0], 'ep', axis=0, tiled=True)  28.1 us
    unnamed x1, blocking collectives  27.5 us
    all_gather x1, blocking collectives, per_device(): meta = lax.all_gather(meta, 'ep', axis=0, tiled=False)  15.7 us
    reduce_scatter x2, waiting for transfers between devices, combine(): return lax.psum_scatter(dense, 'ep', scatter_dimension=0, tiled=True)  14.6 us
    ppermute x6, waiting for transfers between devices, out_to(): lax.ppermute(value, 'cp', [(c, (c + step) % cp_count) for c in range(cp_c...  12.1 us
  transfers between devices with their start and end apart: 16, of which 11 were waited for; matrix products, arithmetic and copies ran while one was open for 23% of the time, Pallas kernels for 0%

profile of v2, /device:TPU:0, one launch (start us, length us, event | category | flops | bytes accessed | tf_op | source)
XLA Modules:
  0.0 391.4 jit_solution(14019815954370119737)
XLA Ops:
  10.1 15.7 %all-gather.3 = f32[8,64,16]{1,2,0:T(8,128)S(1)} all-gather(f32[1,64,16]{1,2,0:T(8,128)S(1)} %maximum_bitcast_fusion), channel_id=2, replica_groups=mesh['cp'=4,'ep'=8] {'ep'}, dimensions={0}, use_global_device_ids=true | all-gather | bytes 36864 | tf_op jit(solution)/shard_map/all_gather | solution.py:33
  27.2 28.1 %all-gather.7.cloned.1.call-done = bf16[1,512,3584]{2,1,0:T(8,128)(2,1)} async-done(((bf16[1,64,3584]{2,1,0:T(8,128)(2,1)}), bf16[1,512,3584]{2,1,0:T(8,128)(2,1)}) %all-gather.7.cloned.1.call-update) | async-done | bytes 3670032 | tf_op jit(solution)/shard_map/all_gather | solution.py:34
  55.3 4.0 %convolution_convert_fusion.4 = bf16[160,3584]{1,0:T(8,128)(2,1)} fusion(bf16[1,512,3584]{2,1,0:T(8,128)(2,1)} %all-gather.7.cloned.1.call-done, s32[512]{0:T(512)S(1)} %eq.157), kind=kOutput, calls=%fused_computation.20 | convolution fusion | flops 587857920 | bytes 4818944 | tf_op jit(solution)/shard_map/dot_general | solution.py:11
  59.3 2.4 collective-permute-start.2
  61.7 1.8 convolution_convert_fusion.6
  63.5 1.8 convolution_convert_fusion.5
  65.3 1.1 collective-permute-start.1
  66.4 0.8 convolution_convert_fusion.7
  67.2 31.1 %all-gather.9.cloned.1.call-done = bf16[1,512,3584]{2,1,0:T(8,128)(2,1)} async-done(((bf16[1,64,3584]{2,1,0:T(8,128)(2,1)}), bf16[1,512,3584]{2,1,0:T(8,128)(2,1)}) %all-gather.9.cloned.1.call-update) | async-done | bytes 3670032 | tf_op jit(solution)/shard_map/all_gather | solution.py:35
  98.4 2.9 convolution_convert_fusion.3
  101.5 1.8 convolution_convert_fusion.1
  103.3 1.8 convolution_convert_fusion.2
  106.0 6.6 %collective-permute-done = bf16[160,3584]{1,0:T(8,128)(2,1)} collective-permute-done((bf16[160,3584]{1,0:T(8,128)(2,1)}, bf16[160,3584]{1,0:T(8,128)(2,1)}, u32[]{:S(2)}, u32[]{:S(2)}) %collective-permute-start) | collective-permute-done | bytes 1146912 | tf_op jit(solution)/shard_map/ppermute | solution.py:41
  112.6 4.7 %collective-permute-done.1 = bf16[160,3584]{1,0:T(8,128)(2,1)} collective-permute-done((bf16[160,3584]{1,0:T(8,128)(2,1)}, bf16[160,3584]{1,0:T(8,128)(2,1)}, u32[]{:S(2)}, u32[]{:S(2)}) %collective-permute-start.1) | collective-permute-done | bytes 1146912 | tf_op jit(solution)/shard_map/ppermute | solution.py:41
  117.4 1.3 constant_dynamic-update-slice_fusion.2
  118.8 1.3 constant_dynamic-update-slice_fusion.1
  120.1 1.5 constant_dynamic-update-slice_fusion
  121.7 4.9 %fusion.10 = f32[640,1024]{1,0:T(8,128)S(1)} fusion(bf16[640,3584]{1,0:T(8,128)(2,1)S(1)} %constant_dynamic-update-slice_fusion, bf16[1,3584,1024]{2,1,0:T(8,128)(2,1)S(1)} %bitcast.61), kind=kOutput, calls=%fused_computation.11 | convolution fusion | flops 4697620480 | bytes 14548992 | tf_op jit(solution)/shard_map/dot_general | solution.py:11
  126.6 4.9 %fusion.6 = f32[640,1024]{1,0:T(8,128)S(1)} fusion(bf16[640,3584]{1,0:T(8,128)(2,1)S(1)} %constant_dynamic-update-slice_fusion, bf16[1,3584,1024]{2,1,0:T(8,128)(2,1)S(1)} %bitcast.59), kind=kOutput, calls=%fused_computation.7 | convolution fusion | flops 4697620480 | bytes 14548992 | tf_op jit(solution)/shard_map/dot_general | solution.py:11
  131.5 1.5 copy-done.16
  133.0 5.9 %fusion.12 = bf16[640,3584]{1,0:T(8,128)(2,1)S(1)} fusion(bf16[1,1024,3584]{2,1,0:T(8,128)(2,1)S(1)} %bitcast.57, f32[640,1024]{1,0:T(8,128)S(1)} %fusion.6, f32[640,1024]{1,0:T(8,128)S(1)} %fusion.10), kind=kOutput, calls=%fused_computation.15 | convolution fusion | flops 4703846400 | bytes 17170432 | tf_op jit(solution)/shard_map/dot_general | solution.py:11
  138.9 1.5 fusion.80
  140.5 0.9 copy-done.2
  141.4 0.8 collective-permute-start.4
  142.2 2.9 collective-permute-start.3
  145.2 1.2 collective-permute-start.7
  146.4 24.1 %collective-permute-done.5 = bf16[160,3584]{1,0:T(8,128)(2,1)S(1)} collective-permute-done((bf16[160,3584]{1,0:T(8,128)(2,1)S(1)}, bf16[160,3584]{1,0:T(8,128)(2,1)S(1)}, u32[]{:S(2)}, u32[]{:S(2)}) %collective-permute-start.5) | collective-permute-done | bytes 1146912 | tf_op jit(solution)/shard_map/ppermute | solution.py:44
  170.5 45.5 %collective-permute-done.4 = bf16[160,3584]{1,0:T(8,128)(2,1)S(1)} collective-permute-done((bf16[160,3584]{1,0:T(8,128)(2,1)S(1)}, bf16[160,3584]{1,0:T(8,128)(2,1)S(1)}, u32[]{:S(2)}, u32[]{:S(2)}) %collective-permute-start.4) | collective-permute-done | bytes 1146912 | tf_op jit(solution)/shard_map/ppermute | solution.py:44
  216.1 2.4 multiply_reduce_fusion
  220.1 2.6 multiply_reduce_fusion.2
  224.3 1.4 select_reduce_fusion.7
  230.5 4.4 %fusion.44 = f32[512,3584]{1,0:T(8,128)S(1)} fusion(bf16[512,640]{1,0:T(8,128)(2,1)S(1)} %get-tuple-element.40, bf16[160,3584]{1,0:T(8,128)(2,1)S(1)} %copy-done.4, bf16[160,3584]{1,0:T(8,128)(2,1)S(1)} %copy-done.6, bf16[160,3584]{1,0:T(8,128)(2,1)} %collective-permute-done.3, bf16[160,3584]{1,0:T(8,128)(2,1)S(1)} %get-tuple-element.35), kind=kOutput, calls=%fused_computation.68 | convolution fusion | flops 2367160320 | bytes 12582912 | tf_op jit(solution)/shard_map/dot_general | solution.py:11
  235.0 5.7 %add_convert_fusion.2 = bf16[512,3584]{1,0:T(8,128)(2,1)} fusion(f32[512,3584]{1,0:T(8,128)S(1)} %fusion.44, bf16[512,640]{1,0:T(8,128)(2,1)S(1)} %get-tuple-element.39, bf16[160,3584]{1,0:T(8,128)(2,1)S(1)} %copy-done.4, bf16[160,3584]{1,0:T(8,128)(2,1)S(1)} %copy-done.6, bf16[160,3584]{1,0:T(8,128)(2,1)} %collective-permute-done.3, ...), kind=kOutput, calls=%fused_computation.14 | convolution fusion | flops 2370830336 | bytes 16252928 | tf_op jit(solution)/shard_map/dot_general | solution.py:11
  241.5 10.1 %fusion = f32[640,1024]{1,0:T(8,128)S(1)} fusion(bf16[1,1024,3584]{2,1,0:T(8,128)(2,1)} %param.13, bf16[160,3584]{1,0:T(8,128)(2,1)} %collective-permute-done.8, bf16[160,3584]{1,0:T(8,128)(2,1)} %collective-permute-done.7, bf16[160,3584]{1,0:T(8,128)(2,1)} %collective-permute-done.6, bf16[160,3584]{1,0:T(8,128)(2,1)S(1)} %convolution_convert_fusion.3), kind=kOutput, calls=%fused_computation.1 | convolution fusion | flops 4715970560 | bytes 14548992 | tf_op jit(solution)/shard_map/dot_general | solution.py:11
  251.6 1.5 copy-done.15
  253.1 10.7 %fusion.4 = f32[640,3584]{1,0:T(8,128)} fusion(bf16[1,3584,1024]{2,1,0:T(8,128)(2,1)} %param.12, f32[640,1024]{1,0:T(8,128)S(1)} %fusion, f32[640,1024]{1,0:T(8,128)S(1)} %copy-done.13), kind=kOutput, calls=%fused_computation.5 | convolution fusion | flops 4701552640 | bytes 21757952 | tf_op jit(solution)/shard_map/dot_general | solution.py:11
  263.8 15.3 %add_convert_fusion = bf16[640,3584]{1,0:T(8,128)(2,1)} fusion(f32[640,3584]{1,0:T(8,128)} %fusion.4, bf16[1,3584,1024]{2,1,0:T(8,128)(2,1)} %param.11, f32[640,1024]{1,0:T(8,128)S(1)} %copy-done.14, f32[640,1024]{1,0:T(8,128)} %copy-done.15, f32[640,1024]{1,0:T(8,128)} %copy-done.16), kind=kOutput, calls=%fused_computation | convolution fusion | flops 4708761600 | bytes 28966912 | tf_op jit(solution)/shard_map/dot_general | solution.py:11
  279.1 2.7 fusion.79
  281.8 1.7 collective-permute-start.11
  283.5 1.5 collective-permute-start.10
  285.1 1.2 collective-permute-start.9
  286.3 24.7 %collective-permute-done.11 = bf16[160,3584]{1,0:T(8,128)(2,1)S(1)} collective-permute-done((bf16[160,3584]{1,0:T(8,128)(2,1)S(1)}, bf16[160,3584]{1,0:T(8,128)(2,1)S(1)}, u32[]{:S(2)}, u32[]{:S(2)}) %collective-permute-start.11) | collective-permute-done | bytes 1146912 | tf_op jit(solution)/shard_map/ppermute | solution.py:44
  311.0 21.4 %collective-permute-done.10 = bf16[160,3584]{1,0:T(8,128)(2,1)S(1)} collective-permute-done((bf16[160,3584]{1,0:T(8,128)(2,1)S(1)}, bf16[160,3584]{1,0:T(8,128)(2,1)S(1)}, u32[]{:S(2)}, u32[]{:S(2)}) %collective-permute-start.10) | collective-permute-done | bytes 1146912 | tf_op jit(solution)/shard_map/ppermute | solution.py:44
  332.5 3.2 fusion.43
  335.7 4.5 %add_convert_fusion.1 = bf16[512,3584]{1,0:T(8,128)(2,1)} fusion(f32[512,3584]{1,0:T(8,128)S(1)} %fusion.43, bf16[512,640]{1,0:T(8,128)(2,1)S(1)} %copy-done.8, bf16[160,3584]{1,0:T(8,128)(2,1)S(1)} %collective-permute-done.11, bf16[160,3584]{1,0:T(8,128)(2,1)S(1)} %collective-permute-done.10, bf16[160,3584]{1,0:T(8,128)(2,1)S(1)} %collective-permute-done.9, ...), kind=kOutput, calls=%fused_computation.13 | convolution fusion | flops 2370830336 | bytes 16252928 | tf_op jit(solution)/shard_map/dot_general | solution.py:11
  341.6 27.5 %all-reduce = f32[8,64,8]{1,2,0:T(8,128)S(1)} all-reduce(f32[8,64,8]{1,2,0:T(8,128)S(1)} %get-tuple-element.47), channel_id=7, replica_groups=mesh['cp'=4,'ep'=8] {'ep'}, use_global_device_ids=true, to_apply=%region_18.19.clone | all-reduce | flops 4096 | bytes 32768
  369.1 1.2 constant_dynamic-slice_fusion
  370.3 14.6 %reduce-scatter.5.cloned.1.call-done = bf16[64,3584]{1,0:T(8,128)(2,1)} async-done(((bf16[512,3584]{1,0:T(8,128)(2,1)}), bf16[64,3584]{1,0:T(8,128)(2,1)}) %reduce-scatter.5.cloned.1.call-update) | async-done | bytes 458768 | tf_op jit(solution)/shard_map/reduce_scatter | solution.py:96
  (97 shorter events, 15.6 us)
Async XLA Ops:
  7.2 48.1 %all-gather.7.cloned.1.call-start = ((), (), s32[]{:S(2)}) async-start(), calls=%async_computation.4 | async-start | bytes 4128768 | tf_op jit(solution)/shard_map/all_gather | solution.py:34
  7.9 90.5 %all-gather.9.cloned.1.call-start = ((), (), s32[]{:S(2)}) async-start(), calls=%async_computation.5 | async-start | bytes 4128768 | tf_op jit(solution)/shard_map/all_gather | solution.py:35
  8.6 361.7 %reduce-scatter.3.cloned.1.call-start = ((), (), s32[]{:S(2)}) async-start(), calls=%async_computation.2 | async-start | bytes 4128768 | tf_op jit(solution)/shard_map/reduce_scatter | solution.py:96
  55.3 6.4 %copy-start = (bf16[1,512,3584]{2,1,0:T(8,128)(2,1)S(1)}, bf16[1,512,3584]{2,1,0:T(8,128)(2,1)}, u32[]{:S(2)}) copy-start(bf16[1,512,3584]{2,1,0:T(8,128)(2,1)} %all-gather.7.cloned.1.call-done) | copy-start | bytes 11010052
  59.3 46.7 %collective-permute-start.2 = (bf16[160,3584]{1,0:T(8,128)(2,1)}, bf16[160,3584]{1,0:T(8,128)(2,1)}, u32[]{:S(2)}, u32[]{:S(2)}) collective-permute-start(bf16[160,3584]{1,0:T(8,128)(2,1)} %convolution_convert_fusion.4), channel_id=1, source_target_pairs={{0,24},{8,0},{16,8},{24,16},{1,25},{9,1},{17,9},{25,17},{2,26},{10... | collective-permute-start | bytes 3440648 | tf_op jit(solution)/shard_map/ppermute | solution.py:41
  63.5 49.1 %collective-permute-start = (bf16[160,3584]{1,0:T(8,128)(2,1)}, bf16[160,3584]{1,0:T(8,128)(2,1)}, u32[]{:S(2)}, u32[]{:S(2)}) collective-permute-start(bf16[160,3584]{1,0:T(8,128)(2,1)} %convolution_convert_fusion.6), channel_id=1, source_target_pairs={{0,8},{8,16},{16,24},{24,0},{1,9},{9,17},{17,25},{25,1},{2,10},{10... | collective-permute-start | bytes 3440648 | tf_op jit(solution)/shard_map/ppermute | solution.py:41
  65.3 52.0 %collective-permute-start.1 = (bf16[160,3584]{1,0:T(8,128)(2,1)}, bf16[160,3584]{1,0:T(8,128)(2,1)}, u32[]{:S(2)}, u32[]{:S(2)}) collective-permute-start(bf16[160,3584]{1,0:T(8,128)(2,1)} %convolution_convert_fusion.5), channel_id=1, source_target_pairs={{0,16},{8,24},{16,0},{24,8},{1,17},{9,25},{17,1},{25,9},{2,18},{10... | collective-permute-start | bytes 3440648 | tf_op jit(solution)/shard_map/ppermute | solution.py:41
  98.4 3.1 copy-start.1
  105.2 16.4 %slice-start.4 = ((s8[7340032]{0:T(1024)(128)(4,1)}), s8[4194304]{0:T(1024)(128)(4,1)S(1)}, s32[]{:S(2)}) async-start(s8[7340032]{0:T(1024)(128)(4,1)} %bitcast.60), calls=%async_computation.10 | async-start | bytes 8388608
  106.0 15.7 %slice-start.5 = ((s8[7340032]{0:T(1024)(128)(4,1)}), s8[3145728]{0:T(1024)(128)(4,1)S(1)}, s32[]{:S(2)}) async-start(s8[7340032]{0:T(1024)(128)(4,1)} %bitcast.60), calls=%async_computation.11 | async-start | bytes 6291456
  120.1 6.5 %slice-start.2 = ((s8[7340032]{0:T(1024)(128)(4,1)}), s8[4194304]{0:T(1024)(128)(4,1)S(1)}, s32[]{:S(2)}) async-start(s8[7340032]{0:T(1024)(128)(4,1)} %bitcast.58), calls=%async_computation.8 | async-start | bytes 8388608
  120.1 12.9 %slice-start = ((s8[7340032]{0:T(1024)(128)(4,1)}), s8[4194304]{0:T(1024)(128)(4,1)S(1)}, s32[]{:S(2)}) async-start(s8[7340032]{0:T(1024)(128)(4,1)} %bitcast.56), calls=%async_computation.6 | async-start | bytes 8388608
  121.6 4.9 %slice-start.3 = ((s8[7340032]{0:T(1024)(128)(4,1)}), s8[3145728]{0:T(1024)(128)(4,1)S(1)}, s32[]{:S(2)}) async-start(s8[7340032]{0:T(1024)(128)(4,1)} %bitcast.58), calls=%async_computation.9 | async-start | bytes 6291456
  121.7 11.3 %slice-start.1 = ((s8[7340032]{0:T(1024)(128)(4,1)}), s8[3145728]{0:T(1024)(128)(4,1)S(1)}, s32[]{:S(2)}) async-start(s8[7340032]{0:T(1024)(128)(4,1)} %bitcast.56), calls=%async_computation.7 | async-start | bytes 6291456
  126.6 4.9 %copy-start.12 = (f32[640,1024]{1,0:T(8,128)}, f32[640,1024]{1,0:T(8,128)S(1)}, u32[]{:S(2)}) copy-start(f32[640,1024]{1,0:T(8,128)S(1)} %fusion.10) | copy-start | bytes 7864324
  131.5 1.5 copy-start.16
  138.9 2.5 copy-start.2
  141.4 29.1 %collective-permute-start.5 = (bf16[160,3584]{1,0:T(8,128)(2,1)S(1)}, bf16[160,3584]{1,0:T(8,128)(2,1)S(1)}, u32[]{:S(2)}, u32[]{:S(2)}) collective-permute-start(bf16[160,3584]{1,0:T(8,128)(2,1)S(1)} %get-tuple-element.36), channel_id=1, source_target_pairs={{24,0},{0,8},{8,16},{16,24},{25,1},{1,9},{9,17},{17,25},{26,2},{2,... | collective-permute-start | bytes 3440648 | tf_op jit(solution)/shard_map/ppermute | solution.py:44
  141.4 74.7 %collective-permute-start.4 = (bf16[160,3584]{1,0:T(8,128)(2,1)S(1)}, bf16[160,3584]{1,0:T(8,128)(2,1)S(1)}, u32[]{:S(2)}, u32[]{:S(2)}) collective-permute-start(bf16[160,3584]{1,0:T(8,128)(2,1)S(1)} %get-tuple-element.37), channel_id=1, source_target_pairs={{16,0},{24,8},{0,16},{8,24},{17,1},{25,9},{1,17},{9,25},{18,2},{26... | collective-permute-start | bytes 3440648 | tf_op jit(solution)/shard_map/ppermute | solution.py:44
  142.2 77.8 %collective-permute-start.3 = (bf16[160,3584]{1,0:T(8,128)(2,1)}, bf16[160,3584]{1,0:T(8,128)(2,1)}, u32[]{:S(2)}, u32[]{:S(2)}) collective-permute-start(bf16[160,3584]{1,0:T(8,128)(2,1)} %get-tuple-element.38), channel_id=1, source_target_pairs={{8,0},{16,8},{24,16},{0,24},{9,1},{17,9},{25,17},{1,25},{10,2},{18... | collective-permute-start | bytes 3440648 | tf_op jit(solution)/shard_map/ppermute | solution.py:44
  145.1 95.6 %collective-permute-start.6 = (bf16[160,3584]{1,0:T(8,128)(2,1)}, bf16[160,3584]{1,0:T(8,128)(2,1)}, u32[]{:S(2)}, u32[]{:S(2)}) collective-permute-start(bf16[160,3584]{1,0:T(8,128)(2,1)} %convolution_convert_fusion.2), channel_id=1, source_target_pairs={{0,8},{8,16},{16,24},{24,0},{1,9},{9,17},{17,25},{25,1},{2,10},{10... | collective-permute-start | bytes 3440648 | tf_op jit(solution)/shard_map/ppermute | solution.py:41
  145.2 96.4 %collective-permute-start.7 = (bf16[160,3584]{1,0:T(8,128)(2,1)}, bf16[160,3584]{1,0:T(8,128)(2,1)}, u32[]{:S(2)}, u32[]{:S(2)}) collective-permute-start(bf16[160,3584]{1,0:T(8,128)(2,1)} %convolution_convert_fusion.1), channel_id=1, source_target_pairs={{0,16},{8,24},{16,0},{24,8},{1,17},{9,25},{17,1},{25,9},{2,18},{10... | collective-permute-start | bytes 3440648 | tf_op jit(solution)/shard_map/ppermute | solution.py:41
  170.5 48.0 %copy-start.3 = (bf16[160,3584]{1,0:T(8,128)(2,1)}, bf16[160,3584]{1,0:T(8,128)(2,1)S(1)}, u32[]{:S(2)}) copy-start(bf16[160,3584]{1,0:T(8,128)(2,1)S(1)} %collective-permute-done.5) | copy-start | bytes 3440644
  170.5 71.0 %collective-permute-start.8 = (bf16[160,3584]{1,0:T(8,128)(2,1)S(1)}, bf16[160,3584]{1,0:T(8,128)(2,1)}, u32[]{:S(2)}, u32[]{:S(2)}) collective-permute-start(bf16[160,3584]{1,0:T(8,128)(2,1)S(1)} %convolution_convert_fusion), channel_id=1, source_target_pairs={{0,24},{8,0},{16,8},{24,16},{1,25},{9,1},{17,9},{25,17},{2,26},{10... | collective-permute-start | bytes 3440648 | tf_op jit(solution)/shard_map/ppermute | solution.py:41
  216.1 2.4 copy-start.5
  228.9 1.3 copy-start.4
  228.9 1.6 copy-start.6
  230.2 4.8 %copy-start.9 = (bf16[512,640]{1,0:T(8,128)(2,1)}, bf16[512,640]{1,0:T(8,128)(2,1)S(1)}, u32[]{:S(2)}) copy-start(bf16[512,640]{1,0:T(8,128)(2,1)S(1)} %get-tuple-element.40) | copy-start | bytes 1966084
  230.2 4.8 %copy-start.7 = (bf16[512,640]{1,0:T(8,128)(2,1)}, bf16[512,640]{1,0:T(8,128)(2,1)S(1)}, u32[]{:S(2)}) copy-start(bf16[512,640]{1,0:T(8,128)(2,1)S(1)} %get-tuple-element.39) | copy-start | bytes 1966084
  240.7 144.1 %reduce-scatter.5.cloned.1.call-start = ((), (), s32[]{:S(2)}) async-start(), calls=%async_computation.3 | async-start | bytes 4128768 | tf_op jit(solution)/shard_map/reduce_scatter | solution.py:96
  240.8 12.4 %copy-start.13 = (f32[640,1024]{1,0:T(8,128)S(1)}, f32[640,1024]{1,0:T(8,128)}, u32[]{:S(2)}) copy-start(f32[640,1024]{1,0:T(8,128)} %copy-done.12) | copy-start | bytes 7864324
  251.6 1.5 copy-start.15
  253.1 10.7 %copy-start.14 = (f32[640,1024]{1,0:T(8,128)S(1)}, f32[640,1024]{1,0:T(8,128)}, u32[]{:S(2)}) copy-start(f32[640,1024]{1,0:T(8,128)} %copy-done.12) | copy-start | bytes 7864324
  279.1 53.4 %copy-start.10 = (bf16[512,640]{1,0:T(8,128)(2,1)S(1)}, bf16[512,640]{1,0:T(8,128)(2,1)}, u32[]{:S(2)}) copy-start(bf16[512,640]{1,0:T(8,128)(2,1)} %copy-done.9) | copy-start | bytes 1966084
  281.8 29.2 %collective-permute-start.11 = (bf16[160,3584]{1,0:T(8,128)(2,1)S(1)}, bf16[160,3584]{1,0:T(8,128)(2,1)S(1)}, u32[]{:S(2)}, u32[]{:S(2)}) collective-permute-start(bf16[160,3584]{1,0:T(8,128)(2,1)S(1)} %get-tuple-element.32), channel_id=1, source_target_pairs={{24,0},{0,8},{8,16},{16,24},{25,1},{1,9},{9,17},{17,25},{26,2},{2,... | collective-permute-start | bytes 3440648 | tf_op jit(solution)/shard_map/ppermute | solution.py:44
  283.5 48.9 %collective-permute-start.10 = (bf16[160,3584]{1,0:T(8,128)(2,1)S(1)}, bf16[160,3584]{1,0:T(8,128)(2,1)S(1)}, u32[]{:S(2)}, u32[]{:S(2)}) collective-permute-start(bf16[160,3584]{1,0:T(8,128)(2,1)S(1)} %get-tuple-element.33), channel_id=1, source_target_pairs={{16,0},{24,8},{0,16},{8,24},{17,1},{25,9},{1,17},{9,25},{18,2},{26... | collective-permute-start | bytes 3440648 | tf_op jit(solution)/shard_map/ppermute | solution.py:44
  285.1 47.4 %collective-permute-start.9 = (bf16[160,3584]{1,0:T(8,128)(2,1)S(1)}, bf16[160,3584]{1,0:T(8,128)(2,1)S(1)}, u32[]{:S(2)}, u32[]{:S(2)}) collective-permute-start(bf16[160,3584]{1,0:T(8,128)(2,1)S(1)} %get-tuple-element.34), channel_id=1, source_target_pairs={{8,0},{16,8},{24,16},{0,24},{9,1},{17,9},{25,17},{1,25},{10,2},{18... | collective-permute-start | bytes 3440648 | tf_op jit(solution)/shard_map/ppermute | solution.py:44
  332.5 3.2 copy-start.8
  340.3 0.7 copy-start.11
Sparse Core Ops, SparseCore 0:
  9.6 45.5 all-gather.6
  56.9 41.3 all-gather.8
  240.8 42.0 reduce-scatter.2
  340.4 44.3 reduce-scatter.4
